TPU v7x, 32 devices: a whole 2x2x4 slice. The times are simulated.
32 devices in a mesh: dp: 4 (over z), fsdp: 8 (over y, x, core).
Axes of the slice: x: 2, y: 2, z: 4, core: 2. Of those that a mesh axis runs over, the one named last changes fastest.
Arguments:
- tokens: bfloat16 [32768, 512], P(('dp', 'fsdp')), may hold values from -6 to 6
- segments: int32 [32768], P(('dp', 'fsdp')), may hold values from -1 to 8, as said below
- cotangent: bfloat16 [32768, 512], P(('dp', 'fsdp')), may hold values from -6 to 6
- w_qkv: bfloat16 [512, 1536], P('fsdp'), may hold values from -0.25 to 0.25
- w_out: bfloat16 [512, 512], P('fsdp'), may hold values from -2 to 2
- w_up: bfloat16 [512, 2048], P('fsdp'), may hold values from -0.25 to 0.25
- w_down: bfloat16 [2048, 512], P('fsdp'), may hold values from -0.125 to 0.125
- q_bias: bfloat16 [512], P('fsdp'), may hold values from -3 to 3
- v_bias: bfloat16 [512], P('fsdp'), may hold values from -3 to 3
- out_bias: bfloat16 [512], P('fsdp'), may hold values from -3 to 3
- up_bias: bfloat16 [2048], P('fsdp'), may hold values from -3 to 3
- down_bias: bfloat16 [512], P('fsdp'), may hold values from -3 to 3
- norm1_gain: bfloat16 [512], P('fsdp'), may hold values from 0.099609375 to 1.8984375
- norm1_bias: bfloat16 [512], P('fsdp'), may hold values from -3 to 3
- norm2_gain: bfloat16 [512], P('fsdp'), may hold values from 0.099609375 to 1.8984375
- norm2_bias: bfloat16 [512], P('fsdp'), may hold values from -3 to 3
Outputs:
- mixed: bfloat16 [32768, 512], P(('dp', 'fsdp'))
- tokens_grad: bfloat16 [32768, 512], P(('dp', 'fsdp'))
- qkv_grad: float32 [512, 1536], P('fsdp')
- out_grad: float32 [512, 512], P('fsdp')
- up_grad: float32 [512, 2048], P('fsdp')
- down_grad: float32 [2048, 512], P('fsdp')
- q_bias_grad: float32 [512], P('fsdp')
- v_bias_grad: float32 [512], P('fsdp')
- out_bias_grad: float32 [512], P('fsdp')
- up_bias_grad: float32 [2048], P('fsdp')
- down_bias_grad: float32 [512], P('fsdp')
- norm1_gain_grad: float32 [512], P('fsdp')
- norm1_bias_grad: float32 [512], P('fsdp')
- norm2_gain_grad: float32 [512], P('fsdp')
- norm2_bias_grad: float32 [512], P('fsdp')
Inputs may be any that keep to these rules, and one draw needn't show every extreme that they name: `segments`: within each device's 1024 slots the images lie from the first slot on in order of their number, and the empty slots (-1) follow them. Image 0 of a device has 512 or 64 tokens, every other image 64, at most one image of a device has 512, and every device holds one image or more. Some device's slots are all full and some device has empty slots.
All inputs are finite; a program needn't handle non-finite values.
Results may differ from a plain program's by a relative error of at most 0.018.
Values may be sent and summed in bfloat16 or wider, within the bound.
No kernel may reach another device: no remote copies, remote signals or barrier semaphores. Data moves between devices by JAX's collectives and lax.ppermute only.
A program may use at most 128 MiB of HBM per device.

v0:
```python
import jax
import jax.numpy as jnp
from jax import lax
from jax.sharding import PartitionSpec as P

D = 512
HEADS = 8
HEAD_DIM = 64
MASKED_SCORE = -1e30
NORM_EPSILON = 1e-05


def layer_norm(values, norm_gain, norm_shift):
    centre = jnp.mean(values, -1, keepdims=True)
    centred = values - centre
    spread = jnp.mean(centred * centred, -1, keepdims=True)
    return centred * lax.rsqrt(spread + NORM_EPSILON) * norm_gain + norm_shift


def gelu_tanh(values):
    return jax.nn.gelu(values, approximate=True)


def take_pair(matrix, pair_index):
    width = 2 * HEAD_DIM
    return matrix[:, pair_index * width : (pair_index + 1) * width].reshape(
        matrix.shape[0], 2, HEAD_DIM
    )


def pair_scores(query_rows, keys_pair, seg_rows, segments):
    scores = (
        jnp.einsum("qhd,khd->hqk", query_rows, keys_pair, preferred_element_type=jnp.float32)
        * 0.125
    )
    same_image = seg_rows[:, None] == segments[None, :]
    return jnp.where(same_image[None], scores, MASKED_SCORE)


def attend_forward(queries, keys_pair, values_pair, segments, block_rows):
    row_count = queries.shape[0]

    def one_block(block_index):
        first_row = block_index * block_rows
        query_rows = lax.dynamic_slice_in_dim(queries, first_row, block_rows, 0)
        seg_rows = lax.dynamic_slice_in_dim(segments, first_row, block_rows, 0)
        scores = pair_scores(query_rows, keys_pair, seg_rows, segments)
        row_max = jnp.max(scores, -1)
        raised = jnp.exp(scores - row_max[..., None])
        row_sums = jnp.sum(raised, -1)
        chances = (raised / row_sums[..., None]).astype(jnp.bfloat16)
        result = jnp.einsum(
            "hqk,khd->qhd", chances, values_pair, preferred_element_type=jnp.float32
        )
        return (result.astype(jnp.bfloat16), row_max + jnp.log(row_sums))

    outputs, log_sums = lax.map(one_block, jnp.arange(row_count // block_rows))
    return (outputs.reshape(row_count, 2 * HEAD_DIM), log_sums)


def attend_backward(queries, keys_pair, values_pair, grad_out, log_sums, segments, block_rows):
    row_count = queries.shape[0]

    def one_block(running, block_index):
        grad_keys, grad_values = running
        first_row = block_index * block_rows
        query_rows = lax.dynamic_slice_in_dim(queries, first_row, block_rows, 0)
        grad_rows = lax.dynamic_slice_in_dim(grad_out, first_row, block_rows, 0)
        seg_rows = lax.dynamic_slice_in_dim(segments, first_row, block_rows, 0)
        scores = pair_scores(query_rows, keys_pair, seg_rows, segments)
        chances = jnp.exp(scores - log_sums[block_index][..., None])
        grad_chances = jnp.einsum(
            "qhd,khd->hqk", grad_rows, values_pair, preferred_element_type=jnp.float32
        )
        inner_sum = jnp.sum(chances * grad_chances, -1, keepdims=True)
        grad_scores = (chances * (grad_chances - inner_sum)).astype(jnp.bfloat16)
        grad_queries = (
            jnp.einsum("hqk,khd->qhd", grad_scores, keys_pair, preferred_element_type=jnp.float32)
            * 0.125
        )
        grad_keys = (
            grad_keys
            + jnp.einsum(
                "hqk,qhd->khd", grad_scores, query_rows, preferred_element_type=jnp.float32
            )
            * 0.125
        )
        grad_values = grad_values + jnp.einsum(
            "hqk,qhd->khd",
            chances.astype(jnp.bfloat16),
            grad_rows,
            preferred_element_type=jnp.float32,
        )
        return ((grad_keys, grad_values), grad_queries)

    empty_grad = jnp.zeros(keys_pair.shape, jnp.float32)
    (grad_keys, grad_values), grad_queries = lax.scan(
        one_block, (empty_grad, empty_grad), jnp.arange(row_count // block_rows)
    )
    width = 2 * HEAD_DIM
    return (
        grad_queries.reshape(row_count, width),
        grad_keys.reshape(row_count, width),
        grad_values.reshape(row_count, width),
    )


def on_device(
    tokens,
    segments,
    cotangent,
    w_qkv,
    w_out,
    w_up,
    w_down,
    q_bias,
    v_bias,
    out_bias,
    up_bias,
    down_bias,
    norm1_gain,
    norm1_bias,
    norm2_gain,
    norm2_bias,
):
    (
        full_qkv,
        full_out,
        full_up,
        full_down,
        full_qb,
        full_vb,
        full_ob,
        full_ub,
        full_db,
        gain_one,
        shift_one,
        gain_two,
        shift_two,
    ) = (
        lax.all_gather(w_qkv, "fsdp", axis=0, tiled=True),
        lax.all_gather(w_out, "fsdp", axis=0, tiled=True),
        lax.all_gather(w_up, "fsdp", axis=0, tiled=True),
        lax.all_gather(w_down, "fsdp", axis=0, tiled=True),
        lax.all_gather(q_bias, "fsdp", axis=0, tiled=True),
        lax.all_gather(v_bias, "fsdp", axis=0, tiled=True),
        lax.all_gather(out_bias, "fsdp", axis=0, tiled=True),
        lax.all_gather(up_bias, "fsdp", axis=0, tiled=True),
        lax.all_gather(down_bias, "fsdp", axis=0, tiled=True),
        lax.all_gather(norm1_gain, "fsdp", axis=0, tiled=True),
        lax.all_gather(norm1_bias, "fsdp", axis=0, tiled=True),
        lax.all_gather(norm2_gain, "fsdp", axis=0, tiled=True),
        lax.all_gather(norm2_bias, "fsdp", axis=0, tiled=True),
    )
    row_count = tokens.shape[0]
    block_rows = min(512, row_count)
    inputs = tokens.astype(jnp.float32)
    normed, norm_one_back = jax.vjp(
        layer_norm, inputs, gain_one.astype(jnp.float32), shift_one.astype(jnp.float32)
    )
    normed_low = normed.astype(jnp.bfloat16)
    projected = jnp.dot(normed_low, full_qkv, preferred_element_type=jnp.float32)
    queries = (projected[:, :D] + full_qb.astype(jnp.float32)).astype(jnp.bfloat16)
    keys_all = projected[:, D : 2 * D].astype(jnp.bfloat16)
    values_all = (projected[:, 2 * D :] + full_vb.astype(jnp.float32)).astype(jnp.bfloat16)
    attended_parts = []
    log_parts = []
    for pair_index in range(HEADS // 2):
        out_pair, log_pair = attend_forward(
            take_pair(queries, pair_index),
            take_pair(keys_all, pair_index),
            take_pair(values_all, pair_index),
            segments,
            block_rows,
        )
        attended_parts.append(out_pair)
        log_parts.append(log_pair)
    attended = jnp.concatenate(attended_parts, 1)
    branch = jnp.dot(attended, full_out, preferred_element_type=jnp.float32) + full_ob.astype(
        jnp.float32
    )
    middle = inputs + branch
    normed_two, norm_two_back = jax.vjp(
        layer_norm, middle, gain_two.astype(jnp.float32), shift_two.astype(jnp.float32)
    )
    normed_two_low = normed_two.astype(jnp.bfloat16)
    hidden = jnp.dot(normed_two_low, full_up, preferred_element_type=jnp.float32) + full_ub.astype(
        jnp.float32
    )
    activated, gelu_back = jax.vjp(gelu_tanh, hidden)
    activated_low = activated.astype(jnp.bfloat16)
    result = (
        middle
        + jnp.dot(activated_low, full_down, preferred_element_type=jnp.float32)
        + full_db.astype(jnp.float32)
    )
    live_rows = (segments >= 0)[:, None]
    mixed = jnp.where(live_rows, result, 0.0).astype(jnp.bfloat16)
    back_qkv, back_out, back_up, back_down = (
        lax.all_gather(w_qkv, "fsdp", axis=0, tiled=True),
        lax.all_gather(w_out, "fsdp", axis=0, tiled=True),
        lax.all_gather(w_up, "fsdp", axis=0, tiled=True),
        lax.all_gather(w_down, "fsdp", axis=0, tiled=True),
    )
    grad_mixed = jnp.where(live_rows, cotangent.astype(jnp.float32), 0.0)
    grad_mlp = grad_mixed.astype(jnp.bfloat16)
    down_grad = jnp.dot(activated_low.T, grad_mlp, preferred_element_type=jnp.float32)
    down_bias_grad = jnp.sum(grad_mlp.astype(jnp.float32), 0)
    (grad_hidden_full,) = gelu_back(
        jnp.dot(grad_mlp, back_down.T, preferred_element_type=jnp.float32)
    )
    grad_hidden = grad_hidden_full.astype(jnp.bfloat16)
    up_grad = jnp.dot(normed_two_low.T, grad_hidden, preferred_element_type=jnp.float32)
    up_bias_grad = jnp.sum(grad_hidden.astype(jnp.float32), 0)
    grad_middle_norm, gain_two_grad, shift_two_grad = norm_two_back(
        jnp.dot(grad_hidden, back_up.T, preferred_element_type=jnp.float32)
    )
    grad_middle = grad_mixed + grad_middle_norm
    grad_branch = grad_middle.astype(jnp.bfloat16)
    out_grad = jnp.dot(attended.T, grad_branch, preferred_element_type=jnp.float32)
    out_bias_grad = jnp.sum(grad_branch.astype(jnp.float32), 0)
    grad_attended = jnp.dot(grad_branch, back_out.T, preferred_element_type=jnp.float32).astype(
        jnp.bfloat16
    )
    query_parts = []
    key_parts = []
    value_parts = []
    for pair_index in range(HEADS // 2):
        grad_q_pair, grad_k_pair, grad_v_pair = attend_backward(
            take_pair(queries, pair_index),
            take_pair(keys_all, pair_index),
            take_pair(values_all, pair_index),
            take_pair(grad_attended, pair_index),
            log_parts[pair_index],
            segments,
            block_rows,
        )
        query_parts.append(grad_q_pair)
        key_parts.append(grad_k_pair)
        value_parts.append(grad_v_pair)
    grad_queries = jnp.concatenate(query_parts, 1).astype(jnp.bfloat16)
    grad_keys = jnp.concatenate(key_parts, 1).astype(jnp.bfloat16)
    grad_values = jnp.concatenate(value_parts, 1).astype(jnp.bfloat16)
    grad_project = jnp.concatenate((grad_queries, grad_keys, grad_values), 1)
    qkv_grad = jnp.dot(normed_low.T, grad_project, preferred_element_type=jnp.float32)
    q_bias_grad = jnp.sum(grad_queries.astype(jnp.float32), 0)
    v_bias_grad = jnp.sum(grad_values.astype(jnp.float32), 0)
    grad_inputs_norm, gain_one_grad, shift_one_grad = norm_one_back(
        jnp.dot(grad_project, back_qkv.T, preferred_element_type=jnp.float32)
    )
    tokens_grad = (grad_middle + grad_inputs_norm).astype(jnp.bfloat16)
    owned = (
        lax.psum_scatter(
            qkv_grad.astype(jnp.bfloat16), "fsdp", scatter_dimension=0, tiled=True
        ).astype(jnp.float32),
        lax.psum_scatter(
            out_grad.astype(jnp.bfloat16), "fsdp", scatter_dimension=0, tiled=True
        ).astype(jnp.float32),
        lax.psum_scatter(
            up_grad.astype(jnp.bfloat16), "fsdp", scatter_dimension=0, tiled=True
        ).astype(jnp.float32),
        lax.psum_scatter(
            down_grad.astype(jnp.bfloat16), "fsdp", scatter_dimension=0, tiled=True
        ).astype(jnp.float32),
        lax.psum_scatter(
            q_bias_grad.astype(jnp.bfloat16), "fsdp", scatter_dimension=0, tiled=True
        ).astype(jnp.float32),
        lax.psum_scatter(
            v_bias_grad.astype(jnp.bfloat16), "fsdp", scatter_dimension=0, tiled=True
        ).astype(jnp.float32),
        lax.psum_scatter(
            out_bias_grad.astype(jnp.bfloat16), "fsdp", scatter_dimension=0, tiled=True
        ).astype(jnp.float32),
        lax.psum_scatter(
            up_bias_grad.astype(jnp.bfloat16), "fsdp", scatter_dimension=0, tiled=True
        ).astype(jnp.float32),
        lax.psum_scatter(
            down_bias_grad.astype(jnp.bfloat16), "fsdp", scatter_dimension=0, tiled=True
        ).astype(jnp.float32),
        lax.psum_scatter(
            gain_one_grad.astype(jnp.bfloat16), "fsdp", scatter_dimension=0, tiled=True
        ).astype(jnp.float32),
        lax.psum_scatter(
            shift_one_grad.astype(jnp.bfloat16), "fsdp", scatter_dimension=0, tiled=True
        ).astype(jnp.float32),
        lax.psum_scatter(
            gain_two_grad.astype(jnp.bfloat16), "fsdp", scatter_dimension=0, tiled=True
        ).astype(jnp.float32),
        lax.psum_scatter(
            shift_two_grad.astype(jnp.bfloat16), "fsdp", scatter_dimension=0, tiled=True
        ).astype(jnp.float32),
    )
    (
        qkv_grad,
        out_grad,
        up_grad,
        down_grad,
        q_bias_grad,
        v_bias_grad,
        out_bias_grad,
        up_bias_grad,
        down_bias_grad,
        gain_one_grad,
        shift_one_grad,
        gain_two_grad,
        shift_two_grad,
    ) = owned
    summed = (
        lax.psum(qkv_grad.astype(jnp.bfloat16), "dp").astype(jnp.float32),
        lax.psum(out_grad.astype(jnp.bfloat16), "dp").astype(jnp.float32),
        lax.psum(up_grad.astype(jnp.bfloat16), "dp").astype(jnp.float32),
        lax.psum(down_grad.astype(jnp.bfloat16), "dp").astype(jnp.float32),
        lax.psum(q_bias_grad.astype(jnp.bfloat16), "dp").astype(jnp.float32),
        lax.psum(v_bias_grad.astype(jnp.bfloat16), "dp").astype(jnp.float32),
        lax.psum(out_bias_grad.astype(jnp.bfloat16), "dp").astype(jnp.float32),
        lax.psum(up_bias_grad.astype(jnp.bfloat16), "dp").astype(jnp.float32),
        lax.psum(down_bias_grad.astype(jnp.bfloat16), "dp").astype(jnp.float32),
        lax.psum(gain_one_grad.astype(jnp.bfloat16), "dp").astype(jnp.float32),
        lax.psum(shift_one_grad.astype(jnp.bfloat16), "dp").astype(jnp.float32),
        lax.psum(gain_two_grad.astype(jnp.bfloat16), "dp").astype(jnp.float32),
        lax.psum(shift_two_grad.astype(jnp.bfloat16), "dp").astype(jnp.float32),
    )
    return (
        mixed,
        tokens_grad,
        summed[0],
        summed[1],
        summed[2],
        summed[3],
        summed[4],
        summed[5],
        summed[6],
        summed[7],
        summed[8],
        summed[9],
        summed[10],
        summed[11],
        summed[12],
    )


def solution(mesh):
    in_specs = (
        P(("dp", "fsdp"), None),
        P(("dp", "fsdp")),
        P(("dp", "fsdp"), None),
        P("fsdp", None),
        P("fsdp", None),
        P("fsdp", None),
        P("fsdp", None),
        P("fsdp"),
        P("fsdp"),
        P("fsdp"),
        P("fsdp"),
        P("fsdp"),
        P("fsdp"),
        P("fsdp"),
        P("fsdp"),
        P("fsdp"),
    )
    out_specs = (
        P(("dp", "fsdp"), None),
        P(("dp", "fsdp"), None),
        P("fsdp", None),
        P("fsdp", None),
        P("fsdp", None),
        P("fsdp", None),
        P("fsdp"),
        P("fsdp"),
        P("fsdp"),
        P("fsdp"),
        P("fsdp"),
        P("fsdp"),
        P("fsdp"),
        P("fsdp"),
        P("fsdp"),
    )
    return jax.shard_map(
        on_device, mesh=mesh, in_specs=in_specs, out_specs=out_specs, check_vma=False
    )
```

profile of v0, /device:TPU:0, one launch (start us, length us, event | category | flops | bytes accessed | tf_op | source)
XLA Modules:
  0.0 452.7 jit_solution(4715248812167894305)
XLA Ops:
  19.4 15.5 %all-reduce.18 = (bf16[512]{0:T(512)(128)(2,1)S(1)}, bf16[512]{0:T(512)(128)(2,1)S(1)}, bf16[512]{0:T(512)(128)(2,1)S(1)}, bf16[512]{0:T(512)(128)(2,1)S(1)}, bf...) all-reduce(bf16[512]{0:T(512)(128)(2,1)S(1)} %dynamic-update-slice., ...), channel_id=1, replica_groups=mesh['dp'=4,'fsdp'=8] {'fsdp'}, use_global_device_ids=true, to_apply=%add.1 | all-reduce | flops 3584 | bytes 14336
  36.7 7.8 %all-gather = bf16[8,1,256]{2,1,0:T(2,128)(2,1)S(1)} all-gather(bf16[1,1,256]{2,1,0:T(2,128)(2,1)S(1)} %reshape.580), channel_id=1, replica_groups=mesh['dp'=4,'fsdp'=8] {'fsdp'}, dimensions={0}, use_global_device_ids=true | all-gather | bytes 4608 | tf_op jit(solution)/shard_map/all_gather | solution.py:148
  45.1 11.6 %all_gather.48 = bf16[512,512]{1,0:T(8,128)(2,1)} all-gather(bf16[64,512]{1,0:T(8,128)(2,1)} %param.36), channel_id=1, replica_groups=mesh['dp'=4,'fsdp'=8] {'fsdp'}, dimensions={0}, use_global_device_ids=true | all-gather | bytes 589824 | tf_op jit(solution)/shard_map/all_gather | solution.py:142
  61.0 6.1 %fusion.190 = (bf16[1024,1536]{1,0:T(8,128)(2,1)S(1)}, f32[1024,1536]{1,0:T(8,128)}) fusion(bf16[512,1536]{1,0:T(8,128)(2,1)} %all-gather.5.cloned.1.call-done, bf16[1024,512]{0,1:T(8,128)(2,1)S(1)} %copy.93, f32[512]{0:T(512)S(1)} %convert_element_type.231, f32[512]{0:T(512)S(1)} %convert_element_type.230, f32[1024]{0:T(1024)S(1)} %fusion.174, ...), kind=kOutput, calls=%fused_computation.263 | convolution fusion | flops 1615331328 | bytes 12070912 | tf_op jit(solution)/shard_map/dot_general | solution.py:162
  76.6 11.0 %while.108 = (s32[]{:T(128)}, bf16[2,512,2,64]{1,3,2,0:T(8,128)(2,1)S(1)}, f32[2,2,512]{2,1,0:T(2,128)S(1)}, s32[2]{0:T(128)S(1)}, s32[1024]{0:T(1024)S(1)}, /*i...) while((s32[]{:T(128)}, ...), condition=%wide.region_5.6_spmd, body=%wide.region_2.5_spmd.sunk | while | flops 281607168 | bytes 15509703 | solution.py:57
  89.1 11.5 %while.109 = (s32[]{:T(128)}, bf16[2,512,2,64]{1,3,2,0:T(8,128)(2,1)S(1)}, f32[2,2,512]{2,1,0:T(2,128)S(1)}, s32[2]{0:T(128)S(1)}, s32[1024]{0:T(1024)S(1)}, /*i...) while((s32[]{:T(128)}, ...), condition=%wide.region_9.10_spmd, body=%wide.region_6.9_spmd.sunk | while | flops 281607168 | bytes 15509703 | solution.py:57
  101.6 11.0 %while.110 = (s32[]{:T(128)}, bf16[2,512,2,64]{1,3,2,0:T(8,128)(2,1)S(1)}, f32[2,2,512]{2,1,0:T(2,128)S(1)}, s32[2]{0:T(128)S(1)}, s32[1024]{0:T(1024)S(1)}, /*i...) while((s32[]{:T(128)}, ...), condition=%wide.region_13.14_spmd, body=%wide.region_10.13_spmd.sunk | while | flops 281607168 | bytes 15509703 | solution.py:57
  113.4 11.0 %while.111 = (s32[]{:T(128)}, bf16[2,512,2,64]{1,3,2,0:T(8,128)(2,1)S(1)}, f32[2,2,512]{2,1,0:T(2,128)S(1)}, s32[2]{0:T(128)S(1)}, s32[1024]{0:T(1024)S(1)}, /*i...) while((s32[]{:T(128)}, ...), condition=%wide.region_17.18_spmd, body=%wide.region_14.17_spmd.sunk | while | flops 281607168 | bytes 15509703 | solution.py:57
  127.3 9.5 %multiply_convert_fusion.4 = (bf16[1024,2048]{1,0:T(8,128)(2,1)}, f32[1024,2048]{1,0:T(8,128)}) fusion(f32[2048]{0:T(1024)S(1)} %bitcast.385, bf16[512,2048]{1,0:T(8,128)(2,1)} %all-gather.7.cloned.1.call-done, f32[1024,512]{0,1:T(8,128)S(1)} %get-tuple-element.938, f32[512]{0:T(512)S(1)} %copy-done.95, f32[512]{0:T(512)S(1)} %copy-done.84, ...), kind=kOutput, calls=%fused_computation.185 | convolution fusion | flops 2171076608 | bytes 16797696 | tf_op jit(solution)/shard_map/dot_general | solution.py:187
  136.8 11.2 %fusion.192 = (bf16[2048]{0:T(1024)(128)(2,1)}, bf16[1024,2048]{1,0:T(8,128)(2,1)S(1)}) fusion(f32[1024,2048]{1,0:T(8,128)} %get-tuple-element.940, f32[2048]{0:T(1024)S(1)} %bitcast.386, bf16[2048,512]{1,0:T(8,128)(2,1)} %all-gather.9.cloned.1.call-done, bf16[1024,512]{0,1:T(8,128)(2,1)} %copy.111, pred[1024]{0:T(1024)(128)(4,1)S(1)} %copy-done.88), kind=kOutput, calls=%fused_computation.265 | convolution fusion | flops 2195191808 | bytes 15741952 | tf_op jit(solution)/shard_map/dot_general | solution.py:210
  148.0 4.3 fusion.194
  166.8 20.7 %while.115 = (s32[]{:T(128)}, f32[1024,2,64]{0,2,1:T(8,128)S(1)}, f32[1024,2,64]{0,2,1:T(8,128)}, bf16[2,512,2,64]{1,3,2,0:T(8,128)(2,1)S(1)}, s32[2]{0:T(128)S(...) while((s32[]{:T(128)}, f32[1024,2,64]{0,2,1:T(8,128)S(1)}, ...), condition=%wide.region_33.34_spmd.clone, body=%wide.region_31.33_spmd.clone.sunk | while | flops 688061440 | bytes 41458004 | solution.py:97
  188.6 20.5 %while.112 = (s32[]{:T(128)}, f32[1024,2,64]{0,2,1:T(8,128)S(1)}, f32[1024,2,64]{0,2,1:T(8,128)}, bf16[2,512,2,64]{1,3,2,0:T(8,128)(2,1)S(1)}, s32[2]{0:T(128)S(...) while((s32[]{:T(128)}, f32[1024,2,64]{0,2,1:T(8,128)S(1)}, ...), condition=%wide.region_24.25_spmd.clone, body=%wide.region_22.24_spmd.clone.sunk | while | flops 688061440 | bytes 41458004 | solution.py:97
  211.0 21.3 %while.114 = (s32[]{:T(128)}, f32[1024,2,64]{0,2,1:T(8,128)S(1)}, f32[1024,2,64]{0,2,1:T(8,128)}, bf16[2,512,2,64]{1,3,2,0:T(8,128)(2,1)}, s32[2]{0:T(128)S(1)},...) while((s32[]{:T(128)}, f32[1024,2,64]{0,2,1:T(8,128)S(1)}, ...), condition=%wide.region_30.31_spmd.clone, body=%wide.region_28.30_spmd.clone.sunk | while | flops 688061440 | bytes 44603816 | solution.py:97
  233.6 20.7 %while.113 = (s32[]{:T(128)}, f32[1024,2,64]{0,2,1:T(8,128)S(1)}, f32[1024,2,64]{0,2,1:T(8,128)}, bf16[2,512,2,64]{1,3,2,0:T(8,128)(2,1)S(1)}, s32[2]{0:T(128)S(...) while((s32[]{:T(128)}, f32[1024,2,64]{0,2,1:T(8,128)S(1)}, ...), condition=%wide.region_27.28_spmd.clone, body=%wide.region_25.27_spmd.clone.sunk | while | flops 688061440 | bytes 41458004 | solution.py:97
  262.9 6.0 %convolution_convert_fusion.1 = bf16[512,2048]{1,0:T(8,128)(2,1)} fusion(bf16[1024,2048]{1,0:T(8,128)(2,1)} %copy-done.101, f32[1024,512]{0,1:T(8,128)S(1)} %copy-done.10, f32[512]{0:T(512)S(1)} %copy-done.96, f32[512]{0:T(512)S(1)} %copy-done.85, f32[1024]{0:T(1024)S(1)} %copy-done.82, f32[1024]{0:T(1024)S(1)} %copy-done.76), kind=kOutput, calls=%fused_computation.196 | convolution fusion | flops 2151153664 | bytes 8400896 | tf_op jit(solution)/shard_map/dot_general | solution.py:213
  269.0 6.6 %convolution_convert_fusion = bf16[2048,512]{1,0:T(8,128)(2,1)} fusion(bf16[1024,2048]{1,0:T(8,128)(2,1)} %get-tuple-element.939, bf16[1024,512]{0,1:T(8,128)(2,1)} %copy.111, pred[1024]{0:T(1024)(128)(4,1)S(1)} %copy-done.89), kind=kOutput, calls=%fused_computation.195 | convolution fusion | flops 2150105088 | bytes 7341056 | tf_op jit(solution)/shard_map/dot_general | solution.py:207
  277.2 5.1 %fusion.193 = (bf16[512]{0:T(512)(128)(2,1)S(1)}, f32[1024,512]{1,0:T(8,128)}) fusion(bf16[1024,1536]{0,1:T(8,128)(2,1)} %copy-done.83, bf16[512,1536]{1,0:T(8,128)(2,1)S(1)} %copy-done.42), kind=kOutput, calls=%fused_computation.266 | convolution fusion | flops 1611136512 | bytes 6816768 | tf_op jit(solution)/shard_map/dot_general | solution.py:249
  288.4 24.0 %all-reduce.17 = (bf16[512]{0:T(512)(128)(2,1)S(1)}, bf16[512]{0:T(512)(128)(2,1)S(1)}, bf16[512]{0:T(512)(128)(2,1)S(1)}, bf16[512]{0:T(512)(128)(2,1)S(1)}, bf...) all-reduce(bf16[512]{0:T(512)(128)(2,1)S(1)} %dynamic-update-slice., ...), channel_id=1, replica_groups=mesh['dp'=4,'fsdp'=8] {'fsdp'}, use_global_device_ids=true, to_apply=%add.7 | all-reduce | flops 6656 | bytes 26624
  312.4 33.9 %reduce-scatter.9.cloned.1.call-done = bf16[64,2048]{1,0:T(8,128)(2,1)} async-done(((bf16[512,2048]{1,0:T(8,128)(2,1)}), bf16[64,2048]{1,0:T(8,128)(2,1)}) %reduce-scatter.9.cloned.1.call-update) | async-done | bytes 262160 | tf_op jit(solution)/shard_map/reduce_scatter | solution.py:259
  346.3 44.5 %reduce-scatter.11.cloned.1.call-done = bf16[256,512]{1,0:T(8,128)(2,1)} async-done(((bf16[2048,512]{1,0:T(8,128)(2,1)}), bf16[256,512]{1,0:T(8,128)(2,1)}) %reduce-scatter.11.cloned.1.call-update) | async-done | bytes 262160 | tf_op jit(solution)/shard_map/reduce_scatter | solution.py:262
  390.9 6.8 %select_convert_fusion = bf16[1024,512]{0,1:T(8,128)(2,1)} fusion(f32[1024,512]{0,1:T(8,128)} %copy-done.9, bf16[1024,2048]{1,0:T(8,128)(2,1)} %get-tuple-element.939, bf16[2048,512]{1,0:T(8,128)(2,1)} %all-gather.9.cloned.1.call-done, f32[512]{0:T(512)S(1)} %convert_element_type.243, pred[1024]{0:T(1024)(128)(4,1)S(1)} %copy-done.89), kind=kOutput, calls=%fused_computation.215 | convolution fusion | flops 2149580800 | bytes 9440256 | tf_op jit(solution)/shard_map/dot_general | solution.py:194
  398.4 12.6 %all-reduce.19 = (bf16[64]{0:T(256)(128)(2,1)S(1)}, bf16[64]{0:T(256)(128)(2,1)S(1)}, bf16[64]{0:T(256)(128)(2,1)S(1)}, bf16[256]{0:T(256)(128)(2,1)S(1)}, bf16[...) all-reduce(bf16[64]{0:T(256)(128)(2,1)S(1)} %dynamic-slice.9, ...), channel_id=1, replica_groups=mesh['dp'=4,'fsdp'=8] {'dp'}, use_global_device_ids=true, to_apply=%region_46.47 | all-reduce | flops 768 | bytes 3072 | tf_op jit(solution)/shard_map/psum | solution.py:313
  424.1 14.8 %all-reduce.23.cloned.1.call-done = (bf16[64,1536]{1,0:T(8,128)(2,1)}, bf16[64,512]{1,0:T(8,128)(2,1)}, bf16[64,2048]{1,0:T(8,128)(2,1)}, bf16[256,512]{1,0:T(8,128)(2,1)}) async-done(((bf16[64,1536]{1,0:T(8,128)(2,1)}, bf16[64,512]{1,0:T(8,128)(2,1)}, bf16[64,2048]{1,0:T(8,128)(2,1)}, bf16[256,512]{1,0:T(8,128)(2,1)}), (bf16[64,1536]{1,0:T(8,128)(2,1)}, bf16[64,512]{1,0:T(8,128)(2,1)}, ...) | async-done | bytes 786448 | tf_op jit(solution)/shard_map/psum | solution.py:309
  (546 shorter events, 186.0 us)
Async XLA Ops:
  7.2 52.5 %copy-start.43 = (bf16[1024,512]{1,0:T(8,128)(2,1)S(1)}, bf16[1024,512]{1,0:T(8,128)(2,1)}, u32[]{:S(2)}) copy-start(bf16[1024,512]{1,0:T(8,128)(2,1)} %param.34) | copy-start | bytes 3145732
  7.2 53.8 %all-gather.5.cloned.1.call-start = ((), (), s32[]{:S(2)}) async-start(), calls=%async_computation.4 | async-start | bytes 1769472 | tf_op jit(solution)/shard_map/all_gather | solution.py:141
  7.9 119.3 %all-gather.7.cloned.1.call-start = ((), (), s32[]{:S(2)}) async-start(), calls=%async_computation.5 | async-start | bytes 2359296 | tf_op jit(solution)/shard_map/all_gather | solution.py:143
  8.7 128.1 %all-gather.9.cloned.1.call-start = ((), (), s32[]{:S(2)}) async-start(), calls=%async_computation.6 | async-start | bytes 2359296 | tf_op jit(solution)/shard_map/all_gather | solution.py:144
  9.4 303.0 %reduce-scatter.7.cloned.1.call-start = ((), (), s32[]{:S(2)}) async-start(), calls=%async_computation.8 | async-start | bytes 589824 | tf_op jit(solution)/shard_map/reduce_scatter | solution.py:256
  34.9 32.2 %copy-start.86 = (f32[512]{0:T(512)}, f32[512]{0:T(512)S(1)}, u32[]{:S(2)}) copy-start(f32[512]{0:T(512)S(1)} %convert_element_type.231) | copy-start | bytes 6148
  35.0 32.1 %copy-start.71 = (f32[512]{0:T(512)}, f32[512]{0:T(512)S(1)}, u32[]{:S(2)}) copy-start(f32[512]{0:T(512)S(1)} %convert_element_type.230) | copy-start | bytes 6148
  126.9 31.2 %copy-start.9 = (f32[1024,512]{0,1:T(8,128)}, f32[1024,512]{0,1:T(8,128)S(1)}, u32[]{:S(2)}) copy-start(f32[1024,512]{0,1:T(8,128)S(1)} %get-tuple-element.938) | copy-start | bytes 6291460
  126.9 31.2 %copy-start.75 = (f32[1024]{0:T(1024)}, f32[1024]{0:T(1024)S(1)}, u32[]{:S(2)}) copy-start(f32[1024]{0:T(1024)S(1)} %broadcast_multiply_fusion) | copy-start | bytes 12292
  127.2 30.9 %copy-start.81 = (f32[1024]{0:T(1024)}, f32[1024]{0:T(1024)S(1)}, u32[]{:S(2)}) copy-start(f32[1024]{0:T(1024)S(1)} %fusion.175) | copy-start | bytes 12292
  164.5 147.8 %reduce-scatter.5.cloned.1.call-start = ((), (), s32[]{:S(2)}) async-start(), calls=%async_computation.7 | async-start | bytes 1769472 | tf_op jit(solution)/shard_map/reduce_scatter | solution.py:253
  188.6 22.3 %copy-start.6 = (bf16[1024,2,64]{0,2,1:T(8,128)(2,1)S(1)}, bf16[1024,2,64]{0,2,1:T(8,128)(2,1)}, u32[]{:S(2)}) copy-start(bf16[1024,2,64]{0,2,1:T(8,128)(2,1)} %copy-done.5) | copy-start | bytes 786436
  188.6 22.3 %copy-start.14 = (f32[1024,2,64]{0,2,1:T(8,128)S(1)}, f32[1024,2,64]{0,2,1:T(8,128)}, u32[]{:S(2)}) copy-start(f32[1024,2,64]{0,2,1:T(8,128)} %custom-call.4) | copy-start | bytes 1572868
  210.9 22.6 %copy-start.4 = (bf16[1024,2,64]{0,2,1:T(8,128)(2,1)S(1)}, bf16[1024,2,64]{0,2,1:T(8,128)(2,1)}, u32[]{:S(2)}) copy-start(bf16[1024,2,64]{0,2,1:T(8,128)(2,1)} %copy-done.3) | copy-start | bytes 786436
  210.9 22.6 %copy-start.13 = (f32[1024,2,64]{0,2,1:T(8,128)S(1)}, f32[1024,2,64]{0,2,1:T(8,128)}, u32[]{:S(2)}) copy-start(f32[1024,2,64]{0,2,1:T(8,128)} %custom-call.2) | copy-start | bytes 1572868
  210.9 22.6 %copy-start.21 = (bf16[1024,2,64]{0,2,1:T(8,128)(2,1)S(1)}, bf16[1024,2,64]{0,2,1:T(8,128)(2,1)}, u32[]{:S(2)}) copy-start(bf16[1024,2,64]{0,2,1:T(8,128)(2,1)} %copy-done.20) | copy-start | bytes 786436
  210.9 22.6 %copy-start.23 = (bf16[1024,2,64]{0,2,1:T(8,128)(2,1)S(1)}, bf16[1024,2,64]{0,2,1:T(8,128)(2,1)}, u32[]{:S(2)}) copy-start(bf16[1024,2,64]{0,2,1:T(8,128)(2,1)} %copy-done.22) | copy-start | bytes 786436
  210.9 22.6 %copy-start.33 = (bf16[1024,128]{0,1:T(8,128)(2,1)S(1)}, bf16[1024,128]{0,1:T(8,128)(2,1)}, u32[]{:S(2)}) copy-start(bf16[1024,128]{0,1:T(8,128)(2,1)} %get-tuple-element.924) | copy-start | bytes 786436
  210.9 22.6 %copy-start.68 = (f32[2,2,512]{2,1,0:T(2,128)S(1)}, f32[2,2,512]{2,1,0:T(2,128)}, u32[]{:S(2)}) copy-start(f32[2,2,512]{2,1,0:T(2,128)} %copy-done.67) | copy-start | bytes 24580
  233.5 22.7 %copy-start.40 = (bf16[16,8,2,512]{3,1,2,0:T(8,128)(2,1)}, bf16[16,8,2,512]{3,1,2,0:T(8,128)(2,1)S(1)}, u32[]{:S(2)}) copy-start(bf16[16,8,2,512]{3,1,2,0:T(8,128)(2,1)S(1)} %copy.129) | copy-start | bytes 786436
  262.8 83.5 %reduce-scatter.9.cloned.1.call-start = ((), (), s32[]{:S(2)}) async-start(), calls=%async_computation.9 | async-start | bytes 2359296 | tf_op jit(solution)/shard_map/reduce_scatter | solution.py:259
  268.9 122.0 %reduce-scatter.11.cloned.1.call-start = ((), (), s32[]{:S(2)}) async-start(), calls=%async_computation.10 | async-start | bytes 2359296 | tf_op jit(solution)/shard_map/reduce_scatter | solution.py:262
  275.6 163.3 %all-reduce.23.cloned.1.call-start = ((), (), s32[]{:S(2)}) async-start(), calls=%async_computation.11 | async-start | bytes 1572864 | tf_op jit(solution)/shard_map/psum | solution.py:309
  390.9 27.1 %copy-start.78 = (f32[1024]{0:T(1024)S(1)}, f32[1024]{0:T(1024)}, u32[]{:S(2)}) copy-start(f32[1024]{0:T(1024)} %copy-done.77) | copy-start | bytes 12292
  (97 other events, 417.5 us)
Sparse Core Ops, SparseCore 0:
  9.9 28.4 all-gather.4
  40.3 28.8 all-gather.6
  71.1 27.9 all-gather.8
  164.7 34.2 reduce-scatter.6
  262.9 38.6 reduce-scatter.4
  305.1 41.1 reduce-scatter.8
  349.6 41.2 reduce-scatter.10
  393.6 45.1 all-reduce.22
where the time goes:
time: 457 us; the launch traced here: 453 us
  matrix products  125 us (27%)
  waiting for transfers between devices  95.4 us (21%)
  blocking collectives  71.6 us (16%)
  other arithmetic  58.4 us (13%)
  local copies, waits for them, and re-layouts  55.5 us (12%)
  loops' own time  28.3 us (6%)
  between operations  18.1 us (4%)
    reduce_scatter x1, waiting for transfers between devices, on_device(): lax.psum_scatter(down_grad.astype(jnp.bfloat16), 'fsdp', scatter_dimensio...  44.5 us
    unnamed x2, blocking collectives  39.5 us
    reduce_scatter x1, waiting for transfers between devices, on_device(): lax.psum_scatter(up_grad.astype(jnp.bfloat16), 'fsdp', scatter_dimension=...  33.9 us
    unnamed x235, local copies, waits for them, and re-layouts  26.4 us
    another operation x4, loops' own time, attend_backward(): lax.scan(one_block, (empty_grad, empty_grad), jnp.arange(row_count // blo...  22.3 us
    dot_general x16, matrix products, pair_scores(): jnp.einsum('qhd,khd->hqk', query_rows, keys_pair, preferred_element_type=...  14.8 us
    psum x1, waiting for transfers between devices, on_device(): lax.psum(qkv_grad.astype(jnp.bfloat16), 'dp').astype(jnp.float32)  14.8 us
    dot_general x8, matrix products, one_block(): jnp.einsum('qhd,khd->hqk', grad_rows, values_pair, preferred_element_type...  14.3 us
  transfers between devices with their start and end apart: 8, of which 3 were waited for; matrix products, arithmetic and copies ran while one was open for 44% of the time, Pallas kernels for 0%

commit v1 on v0

--- a/solution.py
+++ b/solution.py
@@ -8,6 +8,22 @@
 HEAD_DIM = 64
 MASKED_SCORE = -1e30
 NORM_EPSILON = 1e-05
+
+
+def collect(x, axis, dim):
+    ways, here, lap = (lax.axis_size(axis), lax.axis_index(axis), x.shape[dim])
+    dims = [n * ways if d == dim else n for d, n in enumerate(x.shape)]
+    full = lax.dynamic_update_slice_in_dim(jnp.zeros(dims, x.dtype), x, here * lap, axis=dim)
+    going_up = going_down = x
+    for far in range(1, ways // 2 + 1):
+        going_up = lax.ppermute(going_up, axis, [(d, (d + 1) % ways) for d in range(ways)])
+        full = lax.dynamic_update_slice_in_dim(full, going_up, (here - far) % ways * lap, axis=dim)
+        if 2 * far < ways:
+            going_down = lax.ppermute(going_down, axis, [(d, (d - 1) % ways) for d in range(ways)])
+            full = lax.dynamic_update_slice_in_dim(
+                full, going_down, (here + far) % ways * lap, axis=dim
+            )
+    return full
 
 
 def layer_norm(values, norm_gain, norm_shift):
@@ -139,7 +155,7 @@
         shift_two,
     ) = (
         lax.all_gather(w_qkv, "fsdp", axis=0, tiled=True),
-        lax.all_gather(w_out, "fsdp", axis=0, tiled=True),
+        collect(w_out, "fsdp", 0),
         lax.all_gather(w_up, "fsdp", axis=0, tiled=True),
         lax.all_gather(w_down, "fsdp", axis=0, tiled=True),
         lax.all_gather(q_bias, "fsdp", axis=0, tiled=True),

time: 457 us -> 478 us (1.046)
  starting transfers between devices: 0.32 us -> 9.14 us
    ppermute x0 -> x7, starting transfers between devices: none -> 8.81 us  [the longest x3 7.98 us: collect(): lax.ppermute(going_down, axis, [(d, (d - 1) % ways) for d in range(ways)])]
    ppermute x0 -> x7, waiting for transfers between devices: none -> 5.27 us  [the longest x4 5.26 us: collect(): lax.ppermute(going_up, axis, [(d, (d + 1) % ways) for d in range(ways)])]
    dynamic_update_slice x0 -> x8, local copies, waits for them, and re-layouts: none -> 5.07 us  [the longest x4 2.53 us: collect(): lax.dynamic_update_slice_in_dim(full, going_up, (here - far) % ways * lap...]
  transfers between devices with their start and end apart: 8 -> 15, of which waited for: 3 -> 6; matrix products, arithmetic and copies ran while one was open for 44% -> 43% of each run, Pallas kernels for 0% -> 0%
where the time goes in v1:
time: 478 us; the launch traced here: 470 us
  matrix products  126 us (26%)
  waiting for transfers between devices  100 us (21%)
  blocking collectives  70.3 us (15%)
  local copies, waits for them, and re-layouts  59.9 us (13%)
  other arithmetic  58.3 us (12%)
  loops' own time  28 us (6%)
  between operations  18.5 us (4%)
  starting transfers between devices  9.14 us (2%)
    reduce_scatter x1, waiting for transfers between devices, on_device(): lax.psum_scatter(down_grad.astype(jnp.bfloat16), 'fsdp', scatter_dimensio...  44.5 us
    unnamed x2, blocking collectives  36.2 us
    reduce_scatter x1, waiting for transfers between devices, on_device(): lax.psum_scatter(up_grad.astype(jnp.bfloat16), 'fsdp', scatter_dimension=...  34.4 us
    unnamed x235, local copies, waits for them, and re-layouts  26.1 us
    another operation x4, loops' own time, attend_backward(): lax.scan(one_block, (empty_grad, empty_grad), jnp.arange(row_count // blo...  21.9 us
    dot_general x16, matrix products, pair_scores(): jnp.einsum('qhd,khd->hqk', query_rows, keys_pair, preferred_element_type=...  14.8 us
    psum x1, waiting for transfers between devices, on_device(): lax.psum(qkv_grad.astype(jnp.bfloat16), 'dp').astype(jnp.float32)  14.7 us
    dot_general x8, matrix products, one_block(): jnp.einsum('qhd,khd->hqk', grad_rows, values_pair, preferred_element_type...  14.3 us
  transfers between devices with their start and end apart: 15, of which 6 were waited for; matrix products, arithmetic and copies ran while one was open for 43% of the time, Pallas kernels for 0%

profile of v1, /device:TPU:0, one launch (start us, length us, event | category | flops | bytes accessed | tf_op | source)
XLA Modules:
  0.0 470.3 jit_solution(15206224904070111575)
XLA Ops:
  12.4 11.5 %all_gather.54 = bf16[512,512]{1,0:T(8,128)(2,1)} all-gather(bf16[64,512]{1,0:T(8,128)(2,1)} %param.36), channel_id=1, replica_groups=mesh['dp'=4,'fsdp'=8] {'fsdp'}, dimensions={0}, use_global_device_ids=true | all-gather | bytes 589824 | tf_op jit(solution)/shard_map/all_gather | solution.py:217
  33.8 13.5 %all-reduce.18 = (bf16[512]{0:T(512)(128)(2,1)S(1)}, bf16[512]{0:T(512)(128)(2,1)S(1)}, bf16[512]{0:T(512)(128)(2,1)S(1)}, bf16[512]{0:T(512)(128)(2,1)S(1)}, bf...) all-reduce(bf16[512]{0:T(512)(128)(2,1)S(1)} %dynamic-update-slice., ...), channel_id=1, replica_groups=mesh['dp'=4,'fsdp'=8] {'fsdp'}, use_global_device_ids=true, to_apply=%add.1 | all-reduce | flops 3584 | bytes 14336
  48.9 9.9 %all-gather = bf16[8,1,256]{2,1,0:T(2,128)(2,1)S(1)} all-gather(bf16[1,1,256]{2,1,0:T(2,128)(2,1)S(1)} %reshape.580), channel_id=1, replica_groups=mesh['dp'=4,'fsdp'=8] {'fsdp'}, dimensions={0}, use_global_device_ids=true | all-gather | bytes 4608 | tf_op jit(solution)/shard_map/all_gather | solution.py:164
  80.0 6.1 %fusion.190 = (bf16[1024,1536]{1,0:T(8,128)(2,1)S(1)}, f32[1024,1536]{1,0:T(8,128)}) fusion(bf16[512,1536]{1,0:T(8,128)(2,1)} %all-gather.5.cloned.1.call-done, bf16[1024,512]{0,1:T(8,128)(2,1)S(1)} %copy.93, f32[512]{0:T(512)S(1)} %convert_element_type.231, f32[512]{0:T(512)S(1)} %convert_element_type.230, f32[1024]{0:T(1024)S(1)} %fusion.174, ...), kind=kOutput, calls=%fused_computation.271 | convolution fusion | flops 1615331328 | bytes 12070912 | tf_op jit(solution)/shard_map/dot_general | solution.py:178
  95.6 11.5 %while.108 = (s32[]{:T(128)}, bf16[2,512,2,64]{1,3,2,0:T(8,128)(2,1)S(1)}, f32[2,2,512]{2,1,0:T(2,128)S(1)}, s32[2]{0:T(128)S(1)}, s32[1024]{0:T(1024)S(1)}, /*i...) while((s32[]{:T(128)}, ...), condition=%wide.region_5.6_spmd, body=%wide.region_2.5_spmd.sunk | while | flops 281607168 | bytes 15509703 | solution.py:73
  108.5 11.0 %while.109 = (s32[]{:T(128)}, bf16[2,512,2,64]{1,3,2,0:T(8,128)(2,1)S(1)}, f32[2,2,512]{2,1,0:T(2,128)S(1)}, s32[2]{0:T(128)S(1)}, s32[1024]{0:T(1024)S(1)}, /*i...) while((s32[]{:T(128)}, ...), condition=%wide.region_9.10_spmd, body=%wide.region_6.9_spmd.sunk | while | flops 281607168 | bytes 15509703 | solution.py:73
  120.5 11.0 %while.110 = (s32[]{:T(128)}, bf16[2,512,2,64]{1,3,2,0:T(8,128)(2,1)S(1)}, f32[2,2,512]{2,1,0:T(2,128)S(1)}, s32[2]{0:T(128)S(1)}, s32[1024]{0:T(1024)S(1)}, /*i...) while((s32[]{:T(128)}, ...), condition=%wide.region_13.14_spmd, body=%wide.region_10.13_spmd.sunk | while | flops 281607168 | bytes 15509703 | solution.py:73
  132.4 11.2 %while.111 = (s32[]{:T(128)}, bf16[2,512,2,64]{1,3,2,0:T(8,128)(2,1)S(1)}, f32[2,2,512]{2,1,0:T(2,128)S(1)}, s32[2]{0:T(128)S(1)}, s32[1024]{0:T(1024)S(1)}, /*i...) while((s32[]{:T(128)}, ...), condition=%wide.region_17.18_spmd, body=%wide.region_14.17_spmd.sunk | while | flops 281607168 | bytes 15509703 | solution.py:73
  147.6 9.5 %multiply_convert_fusion.4 = (bf16[1024,2048]{1,0:T(8,128)(2,1)}, f32[1024,2048]{1,0:T(8,128)}) fusion(f32[2048]{0:T(1024)S(1)} %bitcast.385, bf16[512,2048]{1,0:T(8,128)(2,1)} %all-gather.7.cloned.1.call-done, f32[1024,512]{0,1:T(8,128)S(1)} %get-tuple-element.938, f32[512]{0:T(512)S(1)} %copy-done.95, f32[512]{0:T(512)S(1)} %copy-done.84, ...), kind=kOutput, calls=%fused_computation.185 | convolution fusion | flops 2171076608 | bytes 16797696 | tf_op jit(solution)/shard_map/dot_general | solution.py:203
  157.1 11.5 %fusion.192 = (bf16[2048]{0:T(1024)(128)(2,1)}, bf16[1024,2048]{1,0:T(8,128)(2,1)S(1)}) fusion(f32[1024,2048]{1,0:T(8,128)} %get-tuple-element.940, f32[2048]{0:T(1024)S(1)} %bitcast.386, bf16[2048,512]{1,0:T(8,128)(2,1)} %all-gather.9.cloned.1.call-done, bf16[1024,512]{0,1:T(8,128)(2,1)} %copy.111, pred[1024]{0:T(1024)(128)(4,1)S(1)} %copy-done.88), kind=kOutput, calls=%fused_computation.273 | convolution fusion | flops 2195191808 | bytes 15741952 | tf_op jit(solution)/shard_map/dot_general | solution.py:226
  168.6 4.2 fusion.194
  185.2 20.5 %while.115 = (s32[]{:T(128)}, f32[1024,2,64]{0,2,1:T(8,128)S(1)}, f32[1024,2,64]{0,2,1:T(8,128)}, bf16[2,512,2,64]{1,3,2,0:T(8,128)(2,1)S(1)}, s32[2]{0:T(128)S(...) while((s32[]{:T(128)}, f32[1024,2,64]{0,2,1:T(8,128)S(1)}, ...), condition=%wide.region_33.34_spmd.clone, body=%wide.region_31.33_spmd.clone.sunk | while | flops 688061440 | bytes 41458004 | solution.py:113
  206.9 20.5 %while.112 = (s32[]{:T(128)}, f32[1024,2,64]{0,2,1:T(8,128)S(1)}, f32[1024,2,64]{0,2,1:T(8,128)}, bf16[2,512,2,64]{1,3,2,0:T(8,128)(2,1)S(1)}, s32[2]{0:T(128)S(...) while((s32[]{:T(128)}, f32[1024,2,64]{0,2,1:T(8,128)S(1)}, ...), condition=%wide.region_24.25_spmd.clone, body=%wide.region_22.24_spmd.clone.sunk | while | flops 688061440 | bytes 41458004 | solution.py:113
  229.2 21.0 %while.114 = (s32[]{:T(128)}, f32[1024,2,64]{0,2,1:T(8,128)S(1)}, f32[1024,2,64]{0,2,1:T(8,128)}, bf16[2,512,2,64]{1,3,2,0:T(8,128)(2,1)}, s32[2]{0:T(128)S(1)},...) while((s32[]{:T(128)}, f32[1024,2,64]{0,2,1:T(8,128)S(1)}, ...), condition=%wide.region_30.31_spmd.clone, body=%wide.region_28.30_spmd.clone.sunk | while | flops 688061440 | bytes 44603816 | solution.py:113
  251.6 20.7 %while.113 = (s32[]{:T(128)}, f32[1024,2,64]{0,2,1:T(8,128)S(1)}, f32[1024,2,64]{0,2,1:T(8,128)}, bf16[2,512,2,64]{1,3,2,0:T(8,128)(2,1)S(1)}, s32[2]{0:T(128)S(...) while((s32[]{:T(128)}, f32[1024,2,64]{0,2,1:T(8,128)S(1)}, ...), condition=%wide.region_27.28_spmd.clone, body=%wide.region_25.27_spmd.clone.sunk | while | flops 688061440 | bytes 41458004 | solution.py:113
  281.0 6.0 %convolution_convert_fusion.1 = bf16[512,2048]{1,0:T(8,128)(2,1)} fusion(bf16[1024,2048]{1,0:T(8,128)(2,1)} %copy-done.101, f32[1024,512]{0,1:T(8,128)S(1)} %copy-done.10, f32[512]{0:T(512)S(1)} %copy-done.96, f32[512]{0:T(512)S(1)} %copy-done.85, f32[1024]{0:T(1024)S(1)} %copy-done.82, f32[1024]{0:T(1024)S(1)} %copy-done.76), kind=kOutput, calls=%fused_computation.196 | convolution fusion | flops 2151153664 | bytes 8400896 | tf_op jit(solution)/shard_map/dot_general | solution.py:229
  287.1 6.6 %convolution_convert_fusion = bf16[2048,512]{1,0:T(8,128)(2,1)} fusion(bf16[1024,2048]{1,0:T(8,128)(2,1)} %get-tuple-element.939, bf16[1024,512]{0,1:T(8,128)(2,1)} %copy.111, pred[1024]{0:T(1024)(128)(4,1)S(1)} %copy-done.89), kind=kOutput, calls=%fused_computation.195 | convolution fusion | flops 2150105088 | bytes 7341056 | tf_op jit(solution)/shard_map/dot_general | solution.py:223
  295.3 5.1 %fusion.193 = (bf16[512]{0:T(512)(128)(2,1)S(1)}, f32[1024,512]{1,0:T(8,128)}) fusion(bf16[1024,1536]{0,1:T(8,128)(2,1)} %copy-done.83, bf16[512,1536]{1,0:T(8,128)(2,1)S(1)} %copy-done.42), kind=kOutput, calls=%fused_computation.274 | convolution fusion | flops 1611136512 | bytes 6816768 | tf_op jit(solution)/shard_map/dot_general | solution.py:265
  306.6 22.8 %all-reduce.17 = (bf16[512]{0:T(512)(128)(2,1)S(1)}, bf16[512]{0:T(512)(128)(2,1)S(1)}, bf16[512]{0:T(512)(128)(2,1)S(1)}, bf16[512]{0:T(512)(128)(2,1)S(1)}, bf...) all-reduce(bf16[512]{0:T(512)(128)(2,1)S(1)} %dynamic-update-slice., ...), channel_id=1, replica_groups=mesh['dp'=4,'fsdp'=8] {'fsdp'}, use_global_device_ids=true, to_apply=%add.7 | all-reduce | flops 6656 | bytes 26624
  329.3 34.4 %reduce-scatter.9.cloned.1.call-done = bf16[64,2048]{1,0:T(8,128)(2,1)} async-done(((bf16[512,2048]{1,0:T(8,128)(2,1)}), bf16[64,2048]{1,0:T(8,128)(2,1)}) %reduce-scatter.9.cloned.1.call-update) | async-done | bytes 262160 | tf_op jit(solution)/shard_map/reduce_scatter | solution.py:275
  363.7 44.5 %reduce-scatter.11.cloned.1.call-done = bf16[256,512]{1,0:T(8,128)(2,1)} async-done(((bf16[2048,512]{1,0:T(8,128)(2,1)}), bf16[256,512]{1,0:T(8,128)(2,1)}) %reduce-scatter.11.cloned.1.call-update) | async-done | bytes 262160 | tf_op jit(solution)/shard_map/reduce_scatter | solution.py:278
  408.3 6.8 %select_convert_fusion = bf16[1024,512]{0,1:T(8,128)(2,1)} fusion(f32[1024,512]{0,1:T(8,128)} %copy-done.9, bf16[1024,2048]{1,0:T(8,128)(2,1)} %get-tuple-element.939, bf16[2048,512]{1,0:T(8,128)(2,1)} %all-gather.9.cloned.1.call-done, f32[512]{0:T(512)S(1)} %convert_element_type.243, pred[1024]{0:T(1024)(128)(4,1)S(1)} %copy-done.89), kind=kOutput, calls=%fused_computation.215 | convolution fusion | flops 2149580800 | bytes 9440256 | tf_op jit(solution)/shard_map/dot_general | solution.py:210
  415.7 12.6 %all-reduce.19 = (bf16[64]{0:T(256)(128)(2,1)S(1)}, bf16[64]{0:T(256)(128)(2,1)S(1)}, bf16[64]{0:T(256)(128)(2,1)S(1)}, bf16[256]{0:T(256)(128)(2,1)S(1)}, bf16[...) all-reduce(bf16[64]{0:T(256)(128)(2,1)S(1)} %dynamic-slice.9, ...), channel_id=1, replica_groups=mesh['dp'=4,'fsdp'=8] {'dp'}, use_global_device_ids=true, to_apply=%region_46.47 | all-reduce | flops 768 | bytes 3072 | tf_op jit(solution)/shard_map/psum | solution.py:329
  441.6 14.7 %all-reduce.23.cloned.1.call-done = (bf16[64,1536]{1,0:T(8,128)(2,1)}, bf16[64,512]{1,0:T(8,128)(2,1)}, bf16[64,2048]{1,0:T(8,128)(2,1)}, bf16[256,512]{1,0:T(8,128)(2,1)}) async-done(((bf16[64,1536]{1,0:T(8,128)(2,1)}, bf16[64,512]{1,0:T(8,128)(2,1)}, bf16[64,2048]{1,0:T(8,128)(2,1)}, bf16[256,512]{1,0:T(8,128)(2,1)}), (bf16[64,1536]{1,0:T(8,128)(2,1)}, bf16[64,512]{1,0:T(8,128)(2,1)}, ...) | async-done | bytes 786448 | tf_op jit(solution)/shard_map/psum | solution.py:325
  (569 shorter events, 204.2 us)
Async XLA Ops:
  7.2 54.9 %copy-start.43 = (bf16[1024,512]{1,0:T(8,128)(2,1)S(1)}, bf16[1024,512]{1,0:T(8,128)(2,1)}, u32[]{:S(2)}) copy-start(bf16[1024,512]{1,0:T(8,128)(2,1)} %param.34) | copy-start | bytes 3145732
  7.2 72.8 %all-gather.5.cloned.1.call-start = ((), (), s32[]{:S(2)}) async-start(), calls=%async_computation.4 | async-start | bytes 1769472 | tf_op jit(solution)/shard_map/all_gather | solution.py:157
  7.9 56.3 %copy-start.62 = (bf16[64,512]{1,0:T(8,128)(2,1)S(1)}, bf16[64,512]{1,0:T(8,128)(2,1)}, u32[]{:S(2)}) copy-start(bf16[64,512]{1,0:T(8,128)(2,1)} %param.36) | copy-start | bytes 196612
  7.9 139.7 %all-gather.7.cloned.1.call-start = ((), (), s32[]{:S(2)}) async-start(), calls=%async_computation.5 | async-start | bytes 2359296 | tf_op jit(solution)/shard_map/all_gather | solution.py:159
  8.7 148.4 %all-gather.9.cloned.1.call-start = ((), (), s32[]{:S(2)}) async-start(), calls=%async_computation.6 | async-start | bytes 2359296 | tf_op jit(solution)/shard_map/all_gather | solution.py:160
  8.7 56.2 %collective-permute-start = (bf16[64,512]{1,0:T(8,128)(2,1)}, bf16[64,512]{1,0:T(8,128)(2,1)S(1)}, u32[]{:S(2)}, u32[]{:S(2)}) collective-permute-start(bf16[64,512]{1,0:T(8,128)(2,1)} %param.36), channel_id=1, source_target_pairs={{0,1},{1,2},{2,3},{3,4},{4,5},{5,6},{6,7},{7,0},{8,9},{9,10},{10,1... | collective-permute-start | bytes 196616 | tf_op jit(solution)/shard_map/ppermute | solution.py:19
  9.2 56.0 %collective-permute-start.1 = (bf16[64,512]{1,0:T(8,128)(2,1)}, bf16[64,512]{1,0:T(8,128)(2,1)S(1)}, u32[]{:S(2)}, u32[]{:S(2)}) collective-permute-start(bf16[64,512]{1,0:T(8,128)(2,1)} %param.36), channel_id=1, source_target_pairs={{0,7},{1,0},{2,1},{3,2},{4,3},{5,4},{6,5},{7,6},{8,15},{9,8},{10,9... | collective-permute-start | bytes 196616 | tf_op jit(solution)/shard_map/ppermute | solution.py:22
  12.2 317.1 %reduce-scatter.7.cloned.1.call-start = ((), (), s32[]{:S(2)}) async-start(), calls=%async_computation.8 | async-start | bytes 589824 | tf_op jit(solution)/shard_map/reduce_scatter | solution.py:272
  47.3 38.8 %copy-start.86 = (f32[512]{0:T(512)}, f32[512]{0:T(512)S(1)}, u32[]{:S(2)}) copy-start(f32[512]{0:T(512)S(1)} %convert_element_type.231) | copy-start | bytes 6148
  47.3 38.7 %copy-start.71 = (f32[512]{0:T(512)}, f32[512]{0:T(512)S(1)}, u32[]{:S(2)}) copy-start(f32[512]{0:T(512)S(1)} %convert_element_type.230) | copy-start | bytes 6148
  60.9 25.1 %copy-start = (bf16[1024,512]{0,1:T(8,128)(2,1)}, bf16[1024,512]{0,1:T(8,128)(2,1)S(1)}, u32[]{:S(2)}) copy-start(bf16[1024,512]{0,1:T(8,128)(2,1)S(1)} %copy.93) | copy-start | bytes 3145732
  64.9 4.6 collective-permute-start.2
  65.2 4.3 collective-permute-start.3
  69.5 5.3 %collective-permute-start.4 = (bf16[64,512]{1,0:T(8,128)(2,1)S(1)}, bf16[64,512]{1,0:T(8,128)(2,1)S(1)}, u32[]{:S(2)}, u32[]{:S(2)}) collective-permute-start(bf16[64,512]{1,0:T(8,128)(2,1)S(1)} %collective-permute-done.2), channel_id=1, source_target_pairs={{0,1},{1,2},{2,3},{3,4},{4,5},{5,6},{6,7},{7,0},{8,9},{9,10},{10,1... | collective-permute-start | bytes 196616 | tf_op jit(solution)/shard_map/ppermute | solution.py:19
  69.5 5.9 %collective-permute-start.5 = (bf16[64,512]{1,0:T(8,128)(2,1)S(1)}, bf16[64,512]{1,0:T(8,128)(2,1)S(1)}, u32[]{:S(2)}, u32[]{:S(2)}) collective-permute-start(bf16[64,512]{1,0:T(8,128)(2,1)S(1)} %collective-permute-done.3), channel_id=1, source_target_pairs={{0,7},{1,0},{2,1},{3,2},{4,3},{5,4},{6,5},{7,6},{8,15},{9,8},{10,9... | collective-permute-start | bytes 196616 | tf_op jit(solution)/shard_map/ppermute | solution.py:22
  74.7 4.6 collective-permute-start.6
  147.2 31.5 %copy-start.9 = (f32[1024,512]{0,1:T(8,128)}, f32[1024,512]{0,1:T(8,128)S(1)}, u32[]{:S(2)}) copy-start(f32[1024,512]{0,1:T(8,128)S(1)} %get-tuple-element.938) | copy-start | bytes 6291460
  147.3 31.5 %copy-start.75 = (f32[1024]{0:T(1024)}, f32[1024]{0:T(1024)S(1)}, u32[]{:S(2)}) copy-start(f32[1024]{0:T(1024)S(1)} %broadcast_multiply_fusion) | copy-start | bytes 12292
  147.6 31.2 %copy-start.81 = (f32[1024]{0:T(1024)}, f32[1024]{0:T(1024)S(1)}, u32[]{:S(2)}) copy-start(f32[1024]{0:T(1024)S(1)} %fusion.175) | copy-start | bytes 12292
  183.4 145.9 %reduce-scatter.5.cloned.1.call-start = ((), (), s32[]{:S(2)}) async-start(), calls=%async_computation.7 | async-start | bytes 1769472 | tf_op jit(solution)/shard_map/reduce_scatter | solution.py:269
  280.9 82.9 %reduce-scatter.9.cloned.1.call-start = ((), (), s32[]{:S(2)}) async-start(), calls=%async_computation.9 | async-start | bytes 2359296 | tf_op jit(solution)/shard_map/reduce_scatter | solution.py:275
  287.0 121.3 %reduce-scatter.11.cloned.1.call-start = ((), (), s32[]{:S(2)}) async-start(), calls=%async_computation.10 | async-start | bytes 2359296 | tf_op jit(solution)/shard_map/reduce_scatter | solution.py:278
  293.6 162.6 %all-reduce.23.cloned.1.call-start = ((), (), s32[]{:S(2)}) async-start(), calls=%async_computation.11 | async-start | bytes 1572864 | tf_op jit(solution)/shard_map/psum | solution.py:325
  408.3 27.1 %copy-start.78 = (f32[1024]{0:T(1024)S(1)}, f32[1024]{0:T(1024)}, u32[]{:S(2)}) copy-start(f32[1024]{0:T(1024)} %copy-done.77) | copy-start | bytes 12292
  (104 other events, 644.1 us)
Sparse Core Ops, SparseCore 0:
  9.9 28.7 all-gather.4
  40.6 27.8 all-gather.6
  70.4 27.8 all-gather.8
  183.6 33.5 reduce-scatter.6
  281.0 37.9 reduce-scatter.4
  322.5 41.2 reduce-scatter.8
  367.0 41.1 reduce-scatter.10
  411.0 45.1 all-reduce.22
